TPU v7x, 32 devices: a whole 2x2x4 slice. The times are simulated.
32 devices in a mesh: groups: 2 (over x), facet: 16 (over z, y, core).
Axes of the slice: x: 2, y: 2, z: 4, core: 2. Of those that a mesh axis runs over, the one named last changes fastest.
Arguments:
- sky_strips: bfloat16 [2, 16, 16384], P(None, 'groups', 'facet'), parts along dimension 1, may hold values from -6 to 6
- prolate: float32 [1024], replicated, may hold values from 0.25 to 1
- subgrid_offset: int32 [16], replicated, may hold values from 0 to 16383
- owner: int32 [16], replicated, may hold values from 0 to 15, as said below
- observed: float32 [64, 2, 8, 8192], P(('groups', 'facet')), parts along dimension 0, may hold values from -6 to 6
- vis_uv: float32 [64, 8192], P(('groups', 'facet')), parts along dimension 0, may hold values from 0 to 512
- vis_count: int32 [64], P(('groups', 'facet')), parts along dimension 0, may hold values from 1 to 8192
Outputs:
- residual_vis: bfloat16 [64, 2, 8, 8192], P(('groups', 'facet')), parts along dimension 0
- image_update: float32 [2, 16, 16384], P(None, 'groups', 'facet'), parts along dimension 1
There are 2 independent parts, one for each index of `groups`. A program takes and returns all parts, laid end to end along the dimension named above; an argument that names none is the same for every part. Nothing has to cross between parts.
Inputs may be any that keep to these rules, and one draw needn't show every extreme that they name: `owner`: each index of facet owns at most 2 subgrids, and some index owns exactly 2.
All inputs are finite; a program needn't handle non-finite values.
Results may differ from a plain program's by a relative error of at most 0.01.
Values may be sent and summed in bfloat16 or wider, within the bound.
A program may use at most 64 MiB of HBM per device.

v0:
```python
import functools
import math

import jax
import jax.numpy as jnp
import numpy as np
from jax import lax
from jax.experimental import pallas as pl
from jax.experimental.pallas import tpu as pltpu
from jax.sharding import PartitionSpec as P

POINTS = 512
FINE = 128
COARSE = POINTS // FINE
CHUNK = 512
TWO_PI = 6.283185307179586
SIN = [(-1) ** k * math.pi ** (2 * k + 1) / math.factorial(2 * k + 1) for k in range(7)]
COS = [(-1) ** k * math.pi ** (2 * k) / math.factorial(2 * k) for k in range(7)]


def sincos_turns(turns):
    frac = turns - jnp.floor(turns + 0.5)
    square = frac * frac
    sine = jnp.full_like(square, SIN[-1])
    cosine = jnp.full_like(square, COS[-1])
    for k in range(len(SIN) - 2, -1, -1):
        sine = sine * square + SIN[k]
        cosine = cosine * square + COS[k]
    sine = sine * frac
    return 1.0 - 2.0 * sine * sine, 2.0 * sine * cosine


def mod(value, modulus):
    if modulus & (modulus - 1) == 0:
        return value & (modulus - 1)
    return lax.rem(value, jnp.int32(modulus))


def wide_table(width, points, modulus):
    index = (np.arange(width, dtype=np.int64)[:, None] * np.arange(points)[None, :]) % modulus
    angle = index.astype(np.float32) * np.float32(TWO_PI / modulus)
    return np.concatenate([np.cos(angle), np.sin(angle)], 1)


def iota(shape, dim):
    return lax.broadcasted_iota(jnp.int32, shape, dim)


def slot_scalars(owner, slots):
    count = owner.shape[0]
    names = [owner[s] for s in range(count)]
    found = []
    for s in range(count):
        rank = jnp.int32(0)
        for before in range(s):
            rank = rank + jnp.where(names[before] == names[s], 1, 0)
        found.append(names[s] * slots + rank)
    return found


def build_tables(uv, fine, coarse_cos, coarse_sin):
    slots, total = uv.shape
    for q in range(slots):

        def visit(c, carry):
            where = pl.ds(pl.multiple_of(c * CHUNK, CHUNK), CHUNK)
            turn = jnp.broadcast_to(uv[pl.ds(q, 1), where], (8, CHUNK)) * (1.0 / POINTS)
            row = iota((8, CHUNK), 0)
            steps = jnp.where(
                row < 6, jnp.left_shift(8, jnp.minimum(row, 5)), jnp.where(row == 6, 384, 0)
            )
            base_cos, base_sin = sincos_turns(row.astype(jnp.float32) * turn)
            step_cos, step_sin = sincos_turns(steps.astype(jnp.float32) * turn)
            coarse_cos[q, :, where] = step_cos
            coarse_sin[q, :, where] = step_sin
            tiles = [(base_cos, base_sin)]
            for level in range(4):
                by_cos = step_cos[level : level + 1, :]
                by_sin = step_sin[level : level + 1, :]
                tiles = tiles + [
                    (a * by_cos - b * by_sin, a * by_sin + b * by_cos) for a, b in tiles
                ]
            for k in range(0, 16, 2):
                for part in range(2):
                    pair = jnp.concatenate([tiles[k][part], tiles[k + 1][part]], 0)
                    fine[q, pl.ds(part * FINE + k * 8, 16), where] = pair.astype(jnp.bfloat16)
            return carry

        lax.fori_loop(0, total // CHUNK, visit, 0)


def forward_slot(sky, prolate, offset, table, modulated, raw, turn_cos, turn_sin):
    facets = sky.shape[0]
    rows = sky.shape[2]
    width = sky.shape[3]
    modulus = facets * width
    index = mod(iota((8, width), 1) * offset, modulus)
    cosine, sine = sincos_turns(index.astype(jnp.float32) * (1.0 / modulus))
    cosine = cosine[:rows] * prolate[...]
    sine = sine[:rows] * prolate[...]

    def modulate(f, carry):
        real = sky[f, 0].astype(jnp.float32)
        imag = sky[f, 1].astype(jnp.float32)
        both = jnp.concatenate([real * cosine + imag * sine, imag * cosine - real * sine], 0)
        modulated[f] = both.astype(jnp.bfloat16)
        return carry

    lax.fori_loop(0, facets, modulate, 0)
    raw[...] = jnp.dot(
        modulated[...].reshape(facets * 2 * rows, width),
        table[...],
        preferred_element_type=jnp.float32,
    ).reshape(facets, 2 * rows, 2 * POINTS)
    place = mod(iota((facets, POINTS), 1) + offset, facets) * iota((facets, POINTS), 0)
    cosine, sine = sincos_turns(mod(place, facets).astype(jnp.float32) * (1.0 / facets))
    turn_cos[...] = cosine
    turn_sin[...] = sine

    def add(f, carry):
        sum_re, sum_im = carry
        upper = raw[f, :rows]
        lower = raw[f, rows:]
        real = upper[:, :POINTS] + lower[:, POINTS:]
        imag = lower[:, :POINTS] - upper[:, POINTS:]
        c = turn_cos[pl.ds(f, 1), :]
        s = turn_sin[pl.ds(f, 1), :]
        return sum_re + real * c + imag * s, sum_im + imag * c - real * s

    zero = jnp.zeros((rows, POINTS), jnp.float32)
    real, imag = lax.fori_loop(0, facets, add, (zero, zero))
    scale = 1.0 / math.sqrt(modulus)
    return real * scale, imag * scale


def degrid(q, grid_re, grid_im, live, observed, fine, coarse_cos, coarse_sin, residual):
    rows = grid_re.shape[0]
    total = observed.shape[3]
    parts_re, parts_im = [], []
    for a in range(COARSE):
        re = grid_re[:, a * FINE : (a + 1) * FINE]
        im = grid_im[:, a * FINE : (a + 1) * FINE]
        parts_re.append(jnp.concatenate([re, -im], 1))
        parts_im.append(jnp.concatenate([im, re], 1))
    left = jnp.concatenate(parts_re + parts_im, 0).astype(jnp.bfloat16)
    half = COARSE * rows
    scale = 1.0 / math.sqrt(POINTS)

    def visit(c, carry):
        start = pl.multiple_of(c * CHUNK, CHUNK)
        where = pl.ds(start, CHUNK)
        basis = fine[q, :, where]
        inner = jnp.dot(left, basis, preferred_element_type=jnp.float32)
        model_re = inner[:rows]
        model_im = inner[half : half + rows]
        turns = []
        for a in range(1, COARSE):
            ec = coarse_cos[q, pl.ds(3 + a, 1), where]
            es = coarse_sin[q, pl.ds(3 + a, 1), where]
            turns.append((ec, es))
            re = inner[a * rows : (a + 1) * rows]
            im = inner[half + a * rows : half + (a + 1) * rows]
            model_re = model_re + re * ec - im * es
            model_im = model_im + re * es + im * ec
        alive = iota((rows, CHUNK), 1) + start < live
        res_re = jnp.where(alive, observed[q, 0, :, where] - model_re * scale, 0.0)
        res_im = jnp.where(alive, observed[q, 1, :, where] - model_im * scale, 0.0)
        res_re = res_re.astype(jnp.bfloat16)
        res_im = res_im.astype(jnp.bfloat16)
        residual[q, 0, :, where] = res_re
        residual[q, 1, :, where] = res_im
        res_re = res_re.astype(jnp.float32)
        res_im = res_im.astype(jnp.float32)
        back_re, back_im = [res_re], [res_im]
        for ec, es in turns:
            back_re.append(res_re * ec + res_im * es)
            back_im.append(res_im * ec - res_re * es)
        back = jnp.concatenate(back_re + back_im, 0).astype(jnp.bfloat16)
        return carry + lax.dot_general(
            back, basis, (((1,), (1,)), ((), ())), preferred_element_type=jnp.float32
        )

    found = lax.fori_loop(
        0, total // CHUNK, visit, jnp.zeros((2 * half, 2 * FINE), jnp.float32)
    )
    upper, lower = found[:half], found[half:]
    real = upper[:, :FINE] + lower[:, FINE:]
    imag = lower[:, :FINE] - upper[:, FINE:]
    real = jnp.concatenate([real[a * rows : (a + 1) * rows] for a in range(COARSE)], 1)
    imag = jnp.concatenate([imag[a * rows : (a + 1) * rows] for a in range(COARSE)], 1)
    return jnp.concatenate([real, imag], 0) * (1.0 / math.sqrt(total))


def middle_kernel(
    offsets, owner, counts, sky, prolate, table, observed, uv, residual, update,
    fine, coarse_cos, coarse_sin, modulated, raw, turn_cos, turn_sin,
):
    slots = observed.shape[0]
    me = lax.axis_index("facet")
    build_tables(uv, fine, coarse_cos, coarse_sin)
    found = slot_scalars(owner, slots)
    for q in range(slots):
        offset = jnp.int32(0)
        live = jnp.int32(0)
        for s, slot in enumerate(found):
            here = slot == me * slots + q
            offset = jnp.where(here, offsets[s], offset)
            live = jnp.where(here, counts[q], live)
        real, imag = forward_slot(
            sky, prolate, offset, table, modulated, raw, turn_cos, turn_sin
        )
        result = degrid(
            q, real, imag, live, observed, fine, coarse_cos, coarse_sin, residual
        )
        update[q] = result.astype(jnp.bfloat16)


def lift(me, facets, offsets, owner, prolate, table, updates, image, scratch):
    lifted, back_cos, back_sin, turn_cos, turn_sin, across_cos, across_sin = scratch
    slots = updates.shape[1]
    number = facets * slots
    rows = updates.shape[2] // 2
    width = table.shape[0]
    modulus = width * facets
    found = slot_scalars(owner, slots)
    chosen = jnp.zeros((number, POINTS), jnp.int32)
    row = iota((number, POINTS), 0)
    for s, slot in enumerate(found):
        chosen = jnp.where(row == slot, offsets[s], chosen)
    place = mod(mod(iota((number, POINTS), 1) + chosen, facets) * me, facets)
    turn_cos[...], turn_sin[...] = sincos_turns(place.astype(jnp.float32) * (1.0 / facets))
    for start in range(0, width, POINTS):
        index = mod((iota((number, POINTS), 1) + start) * chosen, modulus)
        cosine, sine = sincos_turns(index.astype(jnp.float32) * (1.0 / modulus))
        across_cos[:, start : start + POINTS] = cosine
        across_sin[:, start : start + POINTS] = sine

    def raise_one(f, carry):
        for q in range(slots):
            at = f * slots + q
            piece = updates[f, q].astype(jnp.float32)
            real, imag = piece[:rows], piece[rows:]
            c = turn_cos[pl.ds(at, 1), :]
            s = turn_sin[pl.ds(at, 1), :]
            both = jnp.concatenate([real * c - imag * s, real * s + imag * c], 0)
            lifted[at] = both.astype(jnp.bfloat16)
        return carry

    lax.fori_loop(0, facets, raise_one, 0)
    left = lifted[...].reshape(number * 2 * rows, POINTS)
    contract = (((1,), (1,)), ((), ()))
    for target, begin in ((back_cos, 0), (back_sin, POINTS)):
        target[...] = lax.dot_general(
            left,
            table[:, begin : begin + POINTS],
            contract,
            preferred_element_type=jnp.float32,
        ).reshape(number, 2 * rows, width)

    def add(at, carry):
        sum_re, sum_im = carry
        real = back_cos[at, :rows] - back_sin[at, rows:]
        imag = back_sin[at, :rows] + back_cos[at, rows:]
        c = across_cos[pl.ds(at, 1), :]
        s = across_sin[pl.ds(at, 1), :]
        return sum_re + real * c - imag * s, sum_im + real * s + imag * c

    zero = jnp.zeros((rows, width), jnp.float32)
    sum_re, sum_im = lax.fori_loop(0, number, add, (zero, zero))
    weight = prolate[...] * (1.0 / math.sqrt(offsets.shape[0] * POINTS))
    image[0] = sum_re * weight
    image[1] = sum_im * weight


def lift_kernel(offsets, owner, prolate, table, updates, image, *scratch):
    lift(
        lax.axis_index("facet"), updates.shape[0], offsets, owner, prolate, table, updates,
        image, scratch,
    )


VMEM = pl.BlockSpec(memory_space=pltpu.VMEM)
SMEM = pl.BlockSpec(memory_space=pltpu.SMEM)


def local(sky_strips, prolate, subgrid_offset, owner, observed, vis_uv, vis_count):
    rows, width = sky_strips.shape[1:]
    facets = lax.axis_size("facet")
    slots, _, _, total = observed.shape
    number = facets * slots
    table = jnp.asarray(wide_table(width, POINTS, width * facets), jnp.bfloat16)
    prolate_row = prolate[None, :]
    params = pltpu.CompilerParams(vmem_limit_bytes=56 * 1024 * 1024)
    f32, bf16 = jnp.float32, jnp.bfloat16
    sky = lax.all_gather(sky_strips, "facet", axis=0)
    residual, update = pl.pallas_call(
        middle_kernel,
        out_shape=(
            jax.ShapeDtypeStruct(observed.shape, bf16),
            jax.ShapeDtypeStruct((slots, 2 * rows, POINTS), bf16),
        ),
        in_specs=[SMEM] * 3 + [VMEM] * 5,
        out_specs=(VMEM, VMEM),
        scratch_shapes=[
            pltpu.VMEM((slots, 2 * FINE, total), bf16),
            pltpu.VMEM((slots, 8, total), f32),
            pltpu.VMEM((slots, 8, total), f32),
            pltpu.VMEM((facets, 2 * rows, width), bf16),
            pltpu.VMEM((facets, 2 * rows, 2 * POINTS), f32),
            pltpu.VMEM((facets, POINTS), f32),
            pltpu.VMEM((facets, POINTS), f32),
        ],
        compiler_params=params,
    )(subgrid_offset, owner, vis_count, sky, prolate_row, table, observed, vis_uv)
    updates = lax.all_gather(update, "facet", axis=0)
    image = pl.pallas_call(
        lift_kernel,
        out_shape=jax.ShapeDtypeStruct((2, rows, width), f32),
        in_specs=[SMEM] * 2 + [VMEM] * 3,
        out_specs=VMEM,
        scratch_shapes=[
            pltpu.VMEM((number, 2 * rows, POINTS), bf16),
            pltpu.VMEM((number, 2 * rows, width), f32),
            pltpu.VMEM((number, 2 * rows, width), f32),
            pltpu.VMEM((number, POINTS), f32),
            pltpu.VMEM((number, POINTS), f32),
            pltpu.VMEM((number, width), f32),
            pltpu.VMEM((number, width), f32),
        ],
        compiler_params=params,
    )(subgrid_offset, owner, prolate_row, table, updates)
    return residual, image


def solution(mesh):
    in_specs = (
        P(None, "groups", "facet"),
        P(),
        P(),
        P(),
        P(("groups", "facet"), None, None, None),
        P(("groups", "facet"), None),
        P(("groups", "facet")),
    )
    out_specs = (P(("groups", "facet"), None, None, None), P(None, "groups", "facet"))
    return jax.shard_map(local, mesh=mesh, in_specs=in_specs, out_specs=out_specs, check_vma=False)
```

profile of v0, /device:TPU:1, one launch (start us, length us, event | category | flops | bytes accessed | tf_op | source)
XLA Modules:
  0.0 71.6 jit_solution(12176257285336506953)
XLA Ops:
  0.6 26.3 %all-gather = bf16[32,8,1024]{2,1,0:T(8,128)(2,1)} all-gather(bf16[2,8,1024]{2,1,0:T(8,128)(2,1)} %param.8), channel_id=2, replica_groups=mesh['groups'=2,'facet'=16] {'facet'}, dimensions={0}, use_global_device_ids=true | all-gather | bytes 557056 | tf_op jit(solution)/shard_map/all_gather | solution.py:295
  26.9 19.1 %shard_map.95 = (bf16[2,2,8,8192]{3,2,1,0:T(8,128)(2,1)}, bf16[2,16,512]{2,1,0:T(8,128)(2,1)}) custom-call(s32[16]{0:T(128)} %offsets.3, s32[16]{0:T(128)} %owner.3, s32[2]{0:T(128)} %counts.1, bf16[16,2,8,1024]{3,2,1,0:T(8,128)(2,1)} %bitcast.4, f32[1,1024]{1,0:T(1,128)} %bitcast.5, bf16[1024,1024]{1,0:T(8,128)(2,1)} %constant.2.clone.table, ...), custom_call_target="tpu_custom_call" | custom-call | tf_op jit(solution)/shard_map/pallas_call | solution.py:296
  46.0 20.5 %all-gather.1 = bf16[32,16,512]{2,1,0:T(8,128)(2,1)} all-gather(bf16[2,16,512]{2,1,0:T(8,128)(2,1)} %get-tuple-element.5), channel_id=3, replica_groups=mesh['groups'=2,'facet'=16] {'facet'}, dimensions={0}, use_global_device_ids=true | all-gather | bytes 557056 | tf_op jit(solution)/shard_map/all_gather | solution.py:315
  66.5 5.1 %shard_map.96 = f32[2,8,1024]{2,1,0:T(8,128)} custom-call(s32[16]{0:T(128)} %offsets.3, s32[16]{0:T(128)} %owner.3, f32[1,1024]{1,0:T(1,128)} %bitcast.6, bf16[1024,1024]{1,0:T(8,128)(2,1)} %constant.2.clone.table, bf16[16,2,16,512]{3,2,1,0:T(8,128)(2,1)} %bitcast.3), custom_call_target="tpu_custom_call" | custom-call | tf_op jit(solution)/shard_map/pallas_call | solution.py:316
where the time goes:
time: 71.9 us; the launch traced here: 71.6 us
  blocking collectives  46.8 us (65%)
  Pallas kernels  24.2 us (34%)
    all_gather x1, blocking collectives, local(): sky = lax.all_gather(sky_strips, 'facet', axis=0)  26.3 us
    all_gather x1, blocking collectives, local(): updates = lax.all_gather(update, 'facet', axis=0)  20.5 us
    pallas_call x1, Pallas kernels, local(): pl.pallas_call(middle_kernel, out_shape=(jax.ShapeDtypeStruct(observed.sh...  19.1 us
    pallas_call x1, Pallas kernels, local(): pl.pallas_call(lift_kernel, out_shape=jax.ShapeDtypeStruct((2, rows, widt...  5.06 us

commit v1 on v0

v1 whole, which is shorter than its diff:
```python
import math

import jax
import jax.numpy as jnp
import numpy as np
from jax import lax
from jax.experimental import pallas as pl
from jax.experimental.pallas import tpu as pltpu
from jax.sharding import PartitionSpec as P

POINTS = 512
FINE = 128
COARSE = POINTS // FINE
CHUNK = 512
TWO_PI = 6.283185307179586
SIN = [(-1) ** k * math.pi ** (2 * k + 1) / math.factorial(2 * k + 1) for k in range(7)]
COS = [(-1) ** k * math.pi ** (2 * k) / math.factorial(2 * k) for k in range(7)]


def sincos_turns(turns):
    frac = turns - jnp.floor(turns + 0.5)
    square = frac * frac
    sine = jnp.full_like(square, SIN[-1])
    cosine = jnp.full_like(square, COS[-1])
    for k in range(len(SIN) - 2, -1, -1):
        sine = sine * square + SIN[k]
        cosine = cosine * square + COS[k]
    sine = sine * frac
    return 1.0 - 2.0 * sine * sine, 2.0 * sine * cosine


def mod(value, modulus):
    if modulus & (modulus - 1) == 0:
        return value & (modulus - 1)
    return lax.rem(value, jnp.int32(modulus))


def wide_table(width, points, modulus):
    index = (np.arange(width, dtype=np.int64)[:, None] * np.arange(points)[None, :]) % modulus
    angle = index.astype(np.float32) * np.float32(TWO_PI / modulus)
    return np.concatenate([np.cos(angle), np.sin(angle)], 1)


def iota(shape, dim):
    return lax.broadcasted_iota(jnp.int32, shape, dim)


def slot_scalars(owner, slots):
    count = owner.shape[0]
    names = [owner[s] for s in range(count)]
    found = []
    for s in range(count):
        rank = jnp.int32(0)
        for before in range(s):
            rank = rank + jnp.where(names[before] == names[s], 1, 0)
        found.append(names[s] * slots + rank)
    return found


def build_tables(q, uv, fine, coarse_cos, coarse_sin):
    total = uv.shape[1]

    def visit(c, carry):
        where = pl.ds(pl.multiple_of(c * CHUNK, CHUNK), CHUNK)
        turn = jnp.broadcast_to(uv[pl.ds(q, 1), where], (8, CHUNK)) * (1.0 / POINTS)
        row = iota((8, CHUNK), 0)
        steps = jnp.where(
            row < 6, jnp.left_shift(8, jnp.minimum(row, 5)), jnp.where(row == 6, 384, 0)
        )
        base_cos, base_sin = sincos_turns(row.astype(jnp.float32) * turn)
        step_cos, step_sin = sincos_turns(steps.astype(jnp.float32) * turn)
        coarse_cos[q, :, where] = step_cos
        coarse_sin[q, :, where] = step_sin
        tiles = [(base_cos, base_sin)]
        for level in range(4):
            by_cos = step_cos[level : level + 1, :]
            by_sin = step_sin[level : level + 1, :]
            tiles = tiles + [
                (a * by_cos - b * by_sin, a * by_sin + b * by_cos) for a, b in tiles
            ]
        for k in range(0, 16, 2):
            for part in range(2):
                pair = jnp.concatenate([tiles[k][part], tiles[k + 1][part]], 0)
                fine[q, pl.ds(part * FINE + k * 8, 16), where] = pair.astype(jnp.bfloat16)
        return carry

    lax.fori_loop(0, total // CHUNK, visit, 0)


def forward_slot(sky, prolate, offset, table, modulated, raw, turn_cos, turn_sin):
    facets = sky.shape[0]
    rows = sky.shape[1] // 2
    width = sky.shape[2]
    modulus = facets * width
    index = mod(iota((8, width), 1) * offset, modulus)
    cosine, sine = sincos_turns(index.astype(jnp.float32) * (1.0 / modulus))
    cosine = cosine[:rows] * prolate[...]
    sine = sine[:rows] * prolate[...]

    def modulate(f, carry):
        strip = sky[f].astype(jnp.float32)
        real, imag = strip[:rows], strip[rows:]
        both = jnp.concatenate([real * cosine + imag * sine, imag * cosine - real * sine], 0)
        modulated[f] = both.astype(jnp.bfloat16)
        return carry

    lax.fori_loop(0, facets, modulate, 0)
    raw[...] = jnp.dot(
        modulated[...].reshape(facets * 2 * rows, width),
        table[...],
        preferred_element_type=jnp.float32,
    ).reshape(facets, 2 * rows, 2 * POINTS)
    place = mod(iota((facets, POINTS), 1) + offset, facets) * iota((facets, POINTS), 0)
    cosine, sine = sincos_turns(mod(place, facets).astype(jnp.float32) * (1.0 / facets))
    turn_cos[...] = cosine
    turn_sin[...] = sine

    def add(f, carry):
        sum_re, sum_im = carry
        upper = raw[f, :rows]
        lower = raw[f, rows:]
        real = upper[:, :POINTS] + lower[:, POINTS:]
        imag = lower[:, :POINTS] - upper[:, POINTS:]
        c = turn_cos[pl.ds(f, 1), :]
        s = turn_sin[pl.ds(f, 1), :]
        return sum_re + real * c + imag * s, sum_im + imag * c - real * s

    zero = jnp.zeros((rows, POINTS), jnp.float32)
    real, imag = lax.fori_loop(0, facets, add, (zero, zero))
    scale = 1.0 / math.sqrt(modulus)
    return real * scale, imag * scale


def degrid(q, grid_re, grid_im, live, observed, fine, coarse_cos, coarse_sin, residual, midway):
    rows = grid_re.shape[0]
    total = observed.shape[3]
    parts_re, parts_im = [], []
    for a in range(COARSE):
        re = grid_re[:, a * FINE : (a + 1) * FINE]
        im = grid_im[:, a * FINE : (a + 1) * FINE]
        parts_re.append(jnp.concatenate([re, -im], 1))
        parts_im.append(jnp.concatenate([im, re], 1))
    left = jnp.concatenate(parts_re + parts_im, 0).astype(jnp.bfloat16)
    half = COARSE * rows
    scale = 1.0 / math.sqrt(POINTS)

    def visit(c, carry):
        start = pl.multiple_of(c * CHUNK, CHUNK)
        where = pl.ds(start, CHUNK)
        basis = fine[q, :, where]
        inner = jnp.dot(left, basis, preferred_element_type=jnp.float32)
        model_re = inner[:rows]
        model_im = inner[half : half + rows]
        turns = []
        for a in range(1, COARSE):
            ec = coarse_cos[q, pl.ds(3 + a, 1), where]
            es = coarse_sin[q, pl.ds(3 + a, 1), where]
            turns.append((ec, es))
            re = inner[a * rows : (a + 1) * rows]
            im = inner[half + a * rows : half + (a + 1) * rows]
            model_re = model_re + re * ec - im * es
            model_im = model_im + re * es + im * ec
        alive = iota((rows, CHUNK), 1) + start < live
        res_re = jnp.where(alive, observed[q, 0, :, where] - model_re * scale, 0.0)
        res_im = jnp.where(alive, observed[q, 1, :, where] - model_im * scale, 0.0)
        rounded = jnp.concatenate([res_re, res_im], 0).astype(jnp.bfloat16)
        residual[q, :, where] = rounded
        rounded = rounded.astype(jnp.float32)
        res_re, res_im = rounded[:rows], rounded[rows:]
        back_re, back_im = [res_re], [res_im]
        for ec, es in turns:
            back_re.append(res_re * ec + res_im * es)
            back_im.append(res_im * ec - res_re * es)
        back = jnp.concatenate(back_re + back_im, 0).astype(jnp.bfloat16)
        return carry + lax.dot_general(
            back, basis, (((1,), (1,)), ((), ())), preferred_element_type=jnp.float32
        )

    steps = total // CHUNK
    found = jnp.zeros((2 * half, 2 * FINE), jnp.float32)
    found = lax.fori_loop(0, steps // 2, visit, found)
    midway()
    found = lax.fori_loop(steps // 2, steps, visit, found)
    upper, lower = found[:half], found[half:]
    real = upper[:, :FINE] + lower[:, FINE:]
    imag = lower[:, :FINE] - upper[:, FINE:]
    real = jnp.concatenate([real[a * rows : (a + 1) * rows] for a in range(COARSE)], 1)
    imag = jnp.concatenate([imag[a * rows : (a + 1) * rows] for a in range(COARSE)], 1)
    return jnp.concatenate([real, imag], 0) * (1.0 / math.sqrt(total))


class Gather:
    def __init__(self, held, send, recv):
        self.held, self.send, self.recv = held, send, recv
        self.facets = held.shape[0]
        self.outer = self.facets // 4
        self.me = lax.axis_index("facet")
        self.z = lax.div(self.me, 4)
        self.y = lax.rem(lax.div(self.me, 2), 2)
        self.c = lax.rem(self.me, 2)
        self.sent = []

    def name(self, step, row, core):
        return lax.rem(self.z + step, self.outer) * 4 + row * 2 + core

    def peers(self):
        along = [self.name(step, self.y, self.c) for step in range(1, self.outer)]
        return along + [self.name(0, 1 - self.y, self.c), self.name(0, self.y, 1 - self.c)]

    def copy(self, block, sem, target):
        return pltpu.make_async_remote_copy(
            src_ref=self.held.at[block],
            dst_ref=self.held.at[block],
            send_sem=sem,
            recv_sem=self.recv.at[block],
            device_id={"facet": target},
            device_id_type=pl.DeviceIdType.MESH,
        )

    def push(self, block, sem, target):
        copy = self.copy(block, sem, target)
        copy.start()
        self.sent.append(copy)

    def arrive(self, block):
        self.copy(block, self.send.at[0, 0], self.me).wait_recv()

    def to_row(self, block):
        self.push(block, self.send.at[1, block], self.name(0, 1 - self.y, self.c))

    def to_core(self, block):
        self.push(block, self.send.at[2, block], self.name(0, self.y, 1 - self.c))

    def start(self):
        for step in range(1, self.outer):
            self.push(self.me, self.send.at[0, step], self.name(step, self.y, self.c))
        self.to_row(self.me)
        self.to_core(self.me)

    def relay_first(self):
        for step in range(self.outer - 1, 0, -1):
            block = self.name(step, self.y, self.c)
            self.arrive(block)
            self.to_row(block)
            self.to_core(block)

    def relay_second(self):
        for step in range(self.outer, 0, -1):
            block = self.name(step, 1 - self.y, self.c)
            self.arrive(block)
            self.to_core(block)

    def finish(self):
        for row in range(2):
            for step in range(self.outer, 0, -1):
                self.arrive(self.name(step, row, 1 - self.c))

    def drain(self):
        for copy in self.sent:
            copy.wait_send()


def lift_slot(q, slots, offsets, found, updates, table, before, scratch):
    lifted, back_cos, back_sin, turn_cos, turn_sin, across_cos, across_sin = scratch
    facets, both, _ = lifted.shape
    rows = both // 2
    width = table.shape[0]
    modulus = width * facets
    me = lax.axis_index("facet")
    chosen = jnp.zeros((facets, POINTS), jnp.int32)
    row = iota((facets, POINTS), 0) * slots + q
    for s, slot in enumerate(found):
        chosen = jnp.where(row == slot, offsets[s], chosen)
    place = mod(mod(iota((facets, POINTS), 1) + chosen, facets) * me, facets)
    turn_cos[...], turn_sin[...] = sincos_turns(place.astype(jnp.float32) * (1.0 / facets))
    for start in range(0, width, POINTS):
        index = mod((iota((facets, POINTS), 1) + start) * chosen, modulus)
        cosine, sine = sincos_turns(index.astype(jnp.float32) * (1.0 / modulus))
        across_cos[:, start : start + POINTS] = cosine
        across_sin[:, start : start + POINTS] = sine
    before()

    def raise_one(f, carry):
        piece = updates[f].astype(jnp.float32)
        real, imag = piece[:rows], piece[rows:]
        c = turn_cos[pl.ds(f, 1), :]
        s = turn_sin[pl.ds(f, 1), :]
        lifted[f] = jnp.concatenate([real * c - imag * s, real * s + imag * c], 0).astype(
            jnp.bfloat16
        )
        return carry

    lax.fori_loop(0, facets, raise_one, 0)
    left = lifted[...].reshape(facets * both, POINTS)
    for target, begin in ((back_cos, 0), (back_sin, POINTS)):
        target[...] = lax.dot_general(
            left,
            table[:, begin : begin + POINTS],
            (((1,), (1,)), ((), ())),
            preferred_element_type=jnp.float32,
        ).reshape(facets, both, width)

    def add(f, carry):
        sum_re, sum_im = carry
        real = back_cos[f, :rows] - back_sin[f, rows:]
        imag = back_sin[f, :rows] + back_cos[f, rows:]
        c = across_cos[pl.ds(f, 1), :]
        s = across_sin[pl.ds(f, 1), :]
        return sum_re + real * c - imag * s, sum_im + real * s + imag * c

    zero = jnp.zeros((rows, width), jnp.float32)
    return lax.fori_loop(0, facets, add, (zero, zero))


def whole_kernel(
    offsets, owner, counts, sky_own, prolate, table_far, observed_far, uv,
    residual_far, image,
    sky, updates, table, observed, residual, fine, coarse_cos, coarse_sin, modulated, raw,
    turn_cos, turn_sin, lifted, back_cos, back_sin, across_cos, across_sin,
    sky_send, sky_recv, update_send, update_recv, local_sem,
):
    slots = observed.shape[0]
    me = lax.axis_index("facet")
    gather = Gather(sky, sky_send, sky_recv)
    back = [
        Gather(updates.at[q], update_send.at[q], update_recv.at[q]) for q in range(slots)
    ]
    load_table = pltpu.make_async_copy(table_far, table, local_sem.at[0])
    load_table.start()
    loads = [
        pltpu.make_async_copy(observed_far.at[q], observed.at[q], local_sem.at[1 + q])
        for q in range(slots)
    ]
    for load in loads:
        load.start()
    barrier = pltpu.get_barrier_semaphore()
    peers = gather.peers()
    for peer in peers:
        pl.semaphore_signal(
            barrier, inc=1, device_id={"facet": peer}, device_id_type=pl.DeviceIdType.MESH
        )
    sky[me] = sky_own[...]
    pl.semaphore_wait(barrier, len(peers))
    gather.start()
    for q in range(slots):
        build_tables(q, uv, fine, coarse_cos, coarse_sin)
        if q == 0:
            gather.relay_first()
        if q == slots - 1:
            gather.relay_second()
    found = slot_scalars(owner, slots)
    load_table.wait()
    gather.finish()
    stores = []
    for q in range(slots):
        offset = jnp.int32(0)
        live = jnp.int32(0)
        for s, slot in enumerate(found):
            here = slot == me * slots + q
            offset = jnp.where(here, offsets[s], offset)
            live = jnp.where(here, counts[q], live)
        real, imag = forward_slot(
            sky, prolate, offset, table, modulated, raw, turn_cos, turn_sin
        )
        if q > 0:
            back[q - 1].relay_first()
        loads[q].wait()
        result = degrid(
            q, real, imag, live, observed, fine, coarse_cos, coarse_sin, residual,
            back[q - 1].relay_second if q > 0 else lambda: None,
        )
        updates[q, me] = result.astype(jnp.bfloat16)
        back[q].start()
        store = pltpu.make_async_copy(residual.at[q], residual_far.at[q], local_sem.at[1 + slots + q])
        store.start()
        stores.append(store)
    scratch = (lifted, back_cos, back_sin, turn_cos, turn_sin, across_cos, across_sin)
    last = back[slots - 1]
    sum_re = sum_im = 0.0
    for q in range(slots):

        def before():
            if q == 0:
                last.relay_first()
            if q == slots - 1:
                last.relay_second()
            back[q].finish()

        part_re, part_im = lift_slot(
            q, slots, offsets, found, updates.at[q], table, before, scratch
        )
        sum_re = sum_re + part_re
        sum_im = sum_im + part_im
    weight = prolate[...] * (1.0 / math.sqrt(offsets.shape[0] * POINTS))
    image[0] = sum_re * weight
    image[1] = sum_im * weight
    gather.drain()
    for one in back:
        one.drain()
    for store in stores:
        store.wait()


VMEM = pl.BlockSpec(memory_space=pltpu.VMEM)
SMEM = pl.BlockSpec(memory_space=pltpu.SMEM)
FAR = pl.BlockSpec(memory_space=pl.ANY)


def local(sky_strips, prolate, subgrid_offset, owner, observed, vis_uv, vis_count):
    rows, width = sky_strips.shape[1:]
    facets = lax.axis_size("facet")
    slots, _, _, total = observed.shape
    both = 2 * rows
    table = jnp.asarray(wide_table(width, POINTS, width * facets), jnp.bfloat16)
    f32, bf16 = jnp.float32, jnp.bfloat16
    residual, image = pl.pallas_call(
        whole_kernel,
        out_shape=(
            jax.ShapeDtypeStruct((slots, both, total), bf16),
            jax.ShapeDtypeStruct((2, rows, width), f32),
        ),
        in_specs=[SMEM] * 3 + [VMEM] * 2 + [FAR] * 2 + [VMEM],
        out_specs=(FAR, VMEM),
        scratch_shapes=[
            pltpu.VMEM((facets, both, width), bf16),
            pltpu.VMEM((slots, facets, both, POINTS), bf16),
            pltpu.VMEM(table.shape, bf16),
            pltpu.VMEM(observed.shape, f32),
            pltpu.VMEM((slots, both, total), bf16),
            pltpu.VMEM((slots, 2 * FINE, total), bf16),
            pltpu.VMEM((slots, 8, total), f32),
            pltpu.VMEM((slots, 8, total), f32),
            pltpu.VMEM((facets, both, width), bf16),
            pltpu.VMEM((facets, both, 2 * POINTS), f32),
            pltpu.VMEM((facets, POINTS), f32),
            pltpu.VMEM((facets, POINTS), f32),
            pltpu.VMEM((facets, both, POINTS), bf16),
            pltpu.VMEM((facets, both, width), f32),
            pltpu.VMEM((facets, both, width), f32),
            pltpu.VMEM((facets, width), f32),
            pltpu.VMEM((facets, width), f32),
            pltpu.SemaphoreType.DMA((3, facets)),
            pltpu.SemaphoreType.DMA((facets,)),
            pltpu.SemaphoreType.DMA((slots, 3, facets)),
            pltpu.SemaphoreType.DMA((slots, facets)),
            pltpu.SemaphoreType.DMA((1 + 2 * slots,)),
        ],
        compiler_params=pltpu.CompilerParams(
            collective_id=0, has_side_effects=True, vmem_limit_bytes=56 * 1024 * 1024
        ),
    )(
        subgrid_offset,
        owner,
        vis_count,
        sky_strips.reshape(both, width),
        prolate[None, :],
        table,
        observed,
        vis_uv,
    )
    return residual.reshape(slots, 2, rows, total), image


def solution(mesh):
    in_specs = (
        P(None, "groups", "facet"),
        P(),
        P(),
        P(),
        P(("groups", "facet"), None, None, None),
        P(("groups", "facet"), None),
        P(("groups", "facet")),
    )
    out_specs = (P(("groups", "facet"), None, None, None), P(None, "groups", "facet"))
    return jax.shard_map(local, mesh=mesh, in_specs=in_specs, out_specs=out_specs, check_vma=False)
```

time: 71.9 us -> 44.6 us (0.62)
  blocking collectives: 46.8 us -> 0 us
  Pallas kernels: 24.2 us -> 40.3 us
  local copies, waits for them, and re-layouts: 0 us -> 3.34 us
    all_gather x2 -> x0, blocking collectives: 46.8 us -> none  [the longest x1 26.3 us: local(): sky = lax.all_gather(sky_strips, 'facet', axis=0)]
    pallas_call x2 -> x1, Pallas kernels: 24.2 us -> 40.3 us  [local(): pl.pallas_call(whole_kernel, out_shape=(jax.ShapeDtypeStruct((slots, both...]
    unnamed x0 -> x2, local copies, waits for them, and re-layouts: none -> 3.34 us
where the time goes in v1:
time: 44.6 us; the launch traced here: 44.3 us
  Pallas kernels  40.3 us (90%)
  local copies, waits for them, and re-layouts  3.34 us (7%)
  between operations  0.64 us (1%)
    pallas_call x1, Pallas kernels, local(): pl.pallas_call(whole_kernel, out_shape=(jax.ShapeDtypeStruct((slots, both...  40.3 us
    unnamed x2, local copies, waits for them, and re-layouts  3.34 us

profile of v1, /device:TPU:1, one launch (start us, length us, event | category | flops | bytes accessed | tf_op | source)
XLA Modules:
  0.0 44.3 jit_solution(10896108693708395472)
XLA Ops:
  0.6 40.3 %shard_map.95 = (bf16[2,16,8192]{2,1,0:T(8,128)(2,1)}, f32[2,8,1024]{2,1,0:T(8,128)}) custom-call(s32[16]{0:T(128)} %offsets.1, s32[16]{0:T(128)} %owner.1, s32[2]{0:T(128)} %counts.1, bf16[16,1024]{1,0:T(8,128)(2,1)} %bitcast.4, f32[1,1024]{1,0:T(1,128)} %bitcast.5, bf16[1024,1024]{1,0:T(8,128)(2,1)} %constant.2.clone.table_far, ...), custom_call_target="tpu_custom_call" | custom-call | tf_op jit(solution)/shard_map/pallas_call | solution.py:416
  41.0 1.9 %copy.12 = bf16[2,2,8,8192]{3,2,1,0:T(8,128)(2,1)} copy(bf16[2,2,8,8192]{3,2,1,0:T(8,128)(2,1)} %bitcast.3) | data formatting | bytes 1048576
  42.9 1.5 %copy.13 = f32[2,8,1024]{2,1,0:T(8,128)} copy(f32[2,8,1024]{2,1,0:T(8,128)} %get-tuple-element.9) | data formatting | bytes 131072

commit v2 on v1

--- a/solution.py
+++ b/solution.py
@@ -1,3 +1,4 @@
+import functools
 import math
 
 import jax
@@ -11,7 +12,8 @@
 POINTS = 512
 FINE = 128
 COARSE = POINTS // FINE
-CHUNK = 512
+CHUNK = 1024
+UNROLL = 4
 TWO_PI = 6.283185307179586
 SIN = [(-1) ** k * math.pi ** (2 * k + 1) / math.factorial(2 * k + 1) for k in range(7)]
 COS = [(-1) ** k * math.pi ** (2 * k) / math.factorial(2 * k) for k in range(7)]
@@ -104,7 +106,7 @@
         modulated[f] = both.astype(jnp.bfloat16)
         return carry
 
-    lax.fori_loop(0, facets, modulate, 0)
+    lax.fori_loop(0, facets, modulate, 0, unroll=4)
     raw[...] = jnp.dot(
         modulated[...].reshape(facets * 2 * rows, width),
         table[...],
@@ -126,7 +128,7 @@
         return sum_re + real * c + imag * s, sum_im + imag * c - real * s
 
     zero = jnp.zeros((rows, POINTS), jnp.float32)
-    real, imag = lax.fori_loop(0, facets, add, (zero, zero))
+    real, imag = lax.fori_loop(0, facets, add, (zero, zero), unroll=4)
     scale = 1.0 / math.sqrt(modulus)
     return real * scale, imag * scale
 
@@ -178,9 +180,9 @@
 
     steps = total // CHUNK
     found = jnp.zeros((2 * half, 2 * FINE), jnp.float32)
-    found = lax.fori_loop(0, steps // 2, visit, found)
+    found = lax.fori_loop(0, steps // 2, visit, found, unroll=UNROLL)
     midway()
-    found = lax.fori_loop(steps // 2, steps, visit, found)
+    found = lax.fori_loop(steps // 2, steps, visit, found, unroll=UNROLL)
     upper, lower = found[:half], found[half:]
     real = upper[:, :FINE] + lower[:, FINE:]
     imag = lower[:, :FINE] - upper[:, FINE:]
@@ -260,11 +262,8 @@
             copy.wait_send()
 
 
-def lift_slot(q, slots, offsets, found, updates, table, before, scratch):
-    lifted, back_cos, back_sin, turn_cos, turn_sin, across_cos, across_sin = scratch
-    facets, both, _ = lifted.shape
-    rows = both // 2
-    width = table.shape[0]
+def lift_phases(q, slots, offsets, found, turn_cos, turn_sin, across_cos, across_sin):
+    facets, width = across_cos.shape
     modulus = width * facets
     me = lax.axis_index("facet")
     chosen = jnp.zeros((facets, POINTS), jnp.int32)
@@ -278,6 +277,13 @@
         cosine, sine = sincos_turns(index.astype(jnp.float32) * (1.0 / modulus))
         across_cos[:, start : start + POINTS] = cosine
         across_sin[:, start : start + POINTS] = sine
+
+
+def lift_slot(updates, table, before, scratch):
+    lifted, back_cos, back_sin, turn_cos, turn_sin, across_cos, across_sin = scratch
+    facets, both, _ = lifted.shape
+    rows = both // 2
+    width = table.shape[0]
     before()
 
     def raise_one(f, carry):
@@ -290,7 +296,7 @@
         )
         return carry
 
-    lax.fori_loop(0, facets, raise_one, 0)
+    lax.fori_loop(0, facets, raise_one, 0, unroll=4)
     left = lifted[...].reshape(facets * both, POINTS)
     for target, begin in ((back_cos, 0), (back_sin, POINTS)):
         target[...] = lax.dot_general(
@@ -309,14 +315,15 @@
         return sum_re + real * c - imag * s, sum_im + real * s + imag * c
 
     zero = jnp.zeros((rows, width), jnp.float32)
-    return lax.fori_loop(0, facets, add, (zero, zero))
+    return lax.fori_loop(0, facets, add, (zero, zero), unroll=4)
 
 
 def whole_kernel(
     offsets, owner, counts, sky_own, prolate, table_far, observed_far, uv,
     residual_far, image,
     sky, updates, table, observed, residual, fine, coarse_cos, coarse_sin, modulated, raw,
-    turn_cos, turn_sin, lifted, back_cos, back_sin, across_cos, across_sin,
+    turn_cos, turn_sin, lifted, back_cos, back_sin,
+    lift_turn_cos, lift_turn_sin, across_cos, across_sin,
     sky_send, sky_recv, update_send, update_recv, local_sem,
 ):
     slots = observed.shape[0]
@@ -342,13 +349,16 @@
     sky[me] = sky_own[...]
     pl.semaphore_wait(barrier, len(peers))
     gather.start()
+    found = slot_scalars(owner, slots)
+    phases = (lift_turn_cos, lift_turn_sin, across_cos, across_sin)
     for q in range(slots):
         build_tables(q, uv, fine, coarse_cos, coarse_sin)
         if q == 0:
             gather.relay_first()
         if q == slots - 1:
             gather.relay_second()
-    found = slot_scalars(owner, slots)
+    for q in range(slots):
+        lift_phases(q, slots, offsets, found, *(ref.at[q] for ref in phases))
     load_table.wait()
     gather.finish()
     stores = []
@@ -374,31 +384,37 @@
         store = pltpu.make_async_copy(residual.at[q], residual_far.at[q], local_sem.at[1 + slots + q])
         store.start()
         stores.append(store)
-    scratch = (lifted, back_cos, back_sin, turn_cos, turn_sin, across_cos, across_sin)
     last = back[slots - 1]
     sum_re = sum_im = 0.0
     for q in range(slots):
 
         def before():
-            if q == 0:
-                last.relay_first()
             if q == slots - 1:
                 last.relay_second()
             back[q].finish()
+            if q == 0 and slots > 1:
+                last.relay_first()
 
         part_re, part_im = lift_slot(
-            q, slots, offsets, found, updates.at[q], table, before, scratch
+            updates.at[q],
+            table,
+            before,
+            (lifted, back_cos, back_sin) + tuple(ref.at[q] for ref in phases),
         )
         sum_re = sum_re + part_re
         sum_im = sum_im + part_im
-    weight = prolate[...] * (1.0 / math.sqrt(offsets.shape[0] * POINTS))
-    image[0] = sum_re * weight
-    image[1] = sum_im * weight
+    image[0] = sum_re
+    image[1] = sum_im
     gather.drain()
     for one in back:
         one.drain()
     for store in stores:
         store.wait()
+
+
+def last_kernel(scale, residual_in, image_in, prolate, residual, image):
+    residual[...] = residual_in[...]
+    image[...] = image_in[...] * (prolate[...] * scale)[None]
 
 
 VMEM = pl.BlockSpec(memory_space=pltpu.VMEM)
@@ -437,8 +453,10 @@
             pltpu.VMEM((facets, both, POINTS), bf16),
             pltpu.VMEM((facets, both, width), f32),
             pltpu.VMEM((facets, both, width), f32),
-            pltpu.VMEM((facets, width), f32),
-            pltpu.VMEM((facets, width), f32),
+            pltpu.VMEM((slots, facets, POINTS), f32),
+            pltpu.VMEM((slots, facets, POINTS), f32),
+            pltpu.VMEM((slots, facets, width), f32),
+            pltpu.VMEM((slots, facets, width), f32),
             pltpu.SemaphoreType.DMA((3, facets)),
             pltpu.SemaphoreType.DMA((facets,)),
             pltpu.SemaphoreType.DMA((slots, 3, facets)),
@@ -458,6 +476,15 @@
         observed,
         vis_uv,
     )
+    residual, image = pl.pallas_call(
+        functools.partial(last_kernel, 1.0 / math.sqrt(subgrid_offset.shape[0] * POINTS)),
+        out_shape=(
+            jax.ShapeDtypeStruct((slots, both, total), bf16),
+            jax.ShapeDtypeStruct((2, rows, width), f32),
+        ),
+        in_specs=[VMEM, VMEM, VMEM],
+        out_specs=(VMEM, VMEM),
+    )(residual, image, prolate[None, :])
     return residual.reshape(slots, 2, rows, total), image
 
 

time: 44.6 us -> 39.5 us (0.89)
  local copies, waits for them, and re-layouts: 3.34 us -> 0 us
  Pallas kernels: 40.3 us -> 38.7 us
    pallas_call x1, Pallas kernels: 40.3 us -> 36.8 us  [local(): pl.pallas_call(whole_kernel, out_shape=(jax.ShapeDtypeStruct((slots, both...]
    unnamed x2 -> x0, local copies, waits for them, and re-layouts: 3.34 us -> none
    pallas_call x0 -> x1, Pallas kernels: none -> 1.92 us  [local(): pl.pallas_call(functools.partial(last_kernel, 1.0 / math.sqrt(subgrid_off...]
where the time goes in v2:
time: 39.5 us; the launch traced here: 39.3 us
  Pallas kernels  38.7 us (98%)
  between operations  0.64 us (2%)
    pallas_call x1, Pallas kernels, local(): pl.pallas_call(whole_kernel, out_shape=(jax.ShapeDtypeStruct((slots, both...  36.8 us
    pallas_call x1, Pallas kernels, local(): pl.pallas_call(functools.partial(last_kernel, 1.0 / math.sqrt(subgrid_off...  1.92 us

profile of v2, /device:TPU:1, one launch (start us, length us, event | category | flops | bytes accessed | tf_op | source)
XLA Modules:
  0.0 39.3 jit_solution(685579393713444513)
XLA Ops:
  0.6 36.8 %shard_map.95 = (bf16[2,16,8192]{2,1,0:T(8,128)(2,1)}, f32[2,8,1024]{2,1,0:T(8,128)}) custom-call(s32[16]{0:T(128)} %offsets.1, s32[16]{0:T(128)} %owner.1, s32[2]{0:T(128)} %counts.1, bf16[16,1024]{1,0:T(8,128)(2,1)} %bitcast.3, f32[1,1024]{1,0:T(1,128)} %bitcast.4, bf16[1024,1024]{1,0:T(8,128)(2,1)} %constant.2.clone.table_far, ...), custom_call_target="tpu_custom_call" | custom-call | tf_op jit(solution)/shard_map/pallas_call | solution.py:432
  37.4 1.9 %shard_map.96 = (bf16[2,16,8192]{2,1,0:T(8,128)(2,1)}, f32[2,8,1024]{2,1,0:T(8,128)}) custom-call(bf16[2,16,8192]{2,1,0:T(8,128)(2,1)} %get-tuple-element.6.residual_in, f32[2,8,1024]{2,1,0:T(8,128)} %get-tuple-element.7.image_in, f32[1,1024]{1,0:T(1,128)} %bitcast.5), custom_call_target="tpu_custom_call" | custom-call | tf_op jit(solution)/shard_map/pallas_call | solution.py:479
